TPU v7x, 512 devices: a whole 4x4x16 slice. The times are simulated.
512 devices in a mesh: seq: 32 (over z_hi, y, core), rep: 4 (over z_lo), tensor: 4 (over x).
Axes of the slice: x: 4, y: 4, z: 16 (z_hi: 4, z_lo: 4; z = z_hi * 4 + z_lo), core: 2. Of those that a mesh axis runs over, the one named last changes fastest.
Arguments:
- key_value_rows: bfloat16 [4, 49152, 8, 256], P('rep', ('seq', 'tensor')), may hold values from -32 to 32
- queries: bfloat16 [4, 64, 64, 128], P('rep', None, 'tensor'), may hold values from -136 to 136
- w_comp: bfloat16 [2048, 512], replicated, may hold values from -0.125 to 0.125
- latent_gain: bfloat16 [512], replicated, may hold values from 0.099609375 to 1.8984375
- w_up: bfloat16 [8, 512, 256], P('tensor'), may hold values from -0.25 to 0.25
- w_out: bfloat16 [8192, 8192], P('tensor', 'seq'), may hold values from -0.0625 to 0.0625
- replica_order: int32 [4], replicated, may hold values from 0 to 3, each once
Outputs:
- decoded: bfloat16 [4, 64, 8192], P('rep', None, 'seq')
Inputs may be any that keep to these rules, and one draw needn't show every extreme that they name: replica_order is a permutation of the prompts.
All inputs are finite; a program needn't handle non-finite values.
Results may differ from a plain program's by a relative error of at most 0.01.
Values may be sent and summed in bfloat16 or wider, within the bound.
A program may use at most 64 MiB of HBM per device.

v0:
```python
import jax
import jax.numpy as jnp
from jax import lax
from jax.sharding import PartitionSpec as P


def compress(rows, weight, gain):
    projected = jnp.dot(rows, weight, preferred_element_type=jnp.float32)
    scale = lax.rsqrt(jnp.mean(projected * projected, axis=-1, keepdims=True) + 1e-06)
    return (projected * scale * gain.astype(jnp.float32)[None]).astype(jnp.bfloat16)


def shards(key_value_rows, queries, w_comp, latent_gain, w_up, w_out, replica_order):
    here = lax.axis_index("rep")
    piece = lax.all_gather(queries, "rep", axis=0, tiled=True)
    chosen = replica_order == here
    picked = jnp.sum(jnp.where(chosen[:, None, None, None], piece.astype(jnp.float32), 0.0), axis=0)
    query = jnp.where(
        jnp.any(chosen), picked.astype(piece.dtype), jnp.zeros(queries.shape[1:], queries.dtype)
    )
    rows = key_value_rows[0]
    tok_rows = rows.shape[0]
    latent_state = compress(rows.reshape(tok_rows, -1), w_comp, latent_gain)
    local_groups = w_up.shape[0]
    complete_up_weight = lax.all_gather(w_up, "tensor", axis=0, tiled=True)
    lifted_every_group = jnp.einsum(
        "qf,kfy->qky", latent_state, complete_up_weight, preferred_element_type=jnp.float32
    ).astype(jnp.bfloat16)
    tensor_count = lax.axis_size("tensor")
    split = lifted_every_group.reshape(
        tok_rows, tensor_count, local_groups, lifted_every_group.shape[-1]
    )
    moved = lax.all_to_all(split, "tensor", split_axis=1, concat_axis=0, tiled=True)
    lifted = moved.reshape(-1, local_groups, lifted_every_group.shape[-1])
    head_size = query.shape[-1]
    new_count = query.shape[0]
    keys = lifted[..., :head_size]
    values = lifted[..., head_size:]
    grouped_heads = query.reshape(new_count, local_groups, -1, head_size)
    scores = jnp.einsum(
        "nghd,tgd->nght", grouped_heads, keys, preferred_element_type=jnp.float32
    ) * head_size ** (-0.5)
    top = lax.pmax(jnp.max(scores, axis=-1), "seq")
    expo = jnp.exp(scores - top[..., None])
    total = jnp.sum(expo, axis=-1)
    weights = expo.astype(jnp.bfloat16)
    summed = jnp.einsum("nght,tgd->nghd", weights, values, preferred_element_type=jnp.float32)
    summed, total = lax.psum((summed, total), "seq")
    attended_values = (summed / total[..., None]).astype(jnp.bfloat16).reshape(new_count, -1)
    partial_output = jnp.dot(attended_values, w_out, preferred_element_type=jnp.float32)
    mixed = lax.psum(partial_output, "tensor").astype(jnp.bfloat16)[None]
    wanted = replica_order[here]
    piece = lax.all_gather(mixed, "rep", axis=0, tiled=True)
    sources = lax.iota(jnp.int32, piece.shape[0])
    chosen = sources == wanted
    picked = jnp.sum(jnp.where(chosen[:, None, None], piece.astype(jnp.float32), 0.0), axis=0)
    reply = jnp.where(
        jnp.any(chosen), picked.astype(piece.dtype), jnp.zeros(mixed.shape[1:], mixed.dtype)
    )
    return reply[None]


def solution(mesh):
    placed = (
        P("rep", ("seq", "tensor"), None, None),
        P("rep", None, "tensor", None),
        P(),
        P(),
        P("tensor", None, None),
        P("tensor", "seq"),
        P(),
    )
    return jax.shard_map(
        shards, mesh=mesh, in_specs=placed, out_specs=P("rep", None, "seq"), check_vma=False
    )
```

profile of v0, /device:TPU:1, one launch (start us, length us, event | category | flops | bytes accessed | tf_op | source)
XLA Modules:
  0.0 574.7 jit_solution(8149440891389177773)
XLA Ops:
  6.5 0.7 all-gather.4.cloned.1.call-update
  7.3 0.7 all-gather.6.cloned.1.call-update
  8.0 1.9 copy.16
  9.9 1.1 multiply_reduce_fusion
  11.0 42.3 %all-gather.4.cloned.1.call-done = bf16[8,512,256]{2,1,0:T(8,128)(2,1)} async-done(((bf16[2,512,256]{2,1,0:T(8,128)(2,1)}), bf16[8,512,256]{2,1,0:T(8,128)(2,1)}) %all-gather.4.cloned.1.call-update) | async-done | bytes 2097168 | tf_op jit(solution)/shard_map/all_gather | solution.py:25
  53.3 3.8 convolution_convert_fusion
  57.1 4.5 all-to-all-start
  61.6 0.6 dynamic_slice.3
  62.2 0.6 fusion.22
  62.8 31.2 %all-gather.6.cloned.1.call-done = bf16[4,64,16,128]{3,2,1,0:T(8,128)(2,1)} async-done(((bf16[1,64,16,128]{3,2,1,0:T(8,128)(2,1)}), bf16[4,64,16,128]{3,2,1,0:T(8,128)(2,1)}) %all-gather.6.cloned.1.call-update) | async-done | bytes 1048592 | tf_op jit(solution)/shard_map/all_gather | solution.py:15
  94.0 1.5 select_reduce_fusion
  95.5 0.7 select_bitcast_fusion
  96.2 1.5 copy.11
  97.7 3.6 bitcast_reduce_fusion
  101.3 85.5 %pmax.7 = f32[64,2,8]{0,2,1:T(8,128)S(1)} all-reduce(f32[64,2,8]{0,2,1:T(8,128)S(1)} %get-tuple-element.9), channel_id=1, replica_groups=mesh['seq'=32,'rep'=4,'tensor'=4] {'seq'}, use_global_device_ids=true, to_apply=%region_5.6 | all-reduce | flops 1024 | bytes 8192 | tf_op jit(solution)/shard_map/pmax | solution.py:43
  186.8 4.9 fusion.7
  191.8 1.3 iota_compare_fusion
  193.0 4.0 fusion.1
  197.1 91.6 %psum.22 = f32[64,2,8]{0,2,1:T(8,128)S(1)} all-reduce(f32[64,2,8]{0,2,1:T(8,128)S(1)} %fusion.1), channel_id=1, replica_groups=mesh['seq'=32,'rep'=4,'tensor'=4] {'seq'}, use_global_device_ids=true, to_apply=%region_8.9 | all-reduce | flops 1024 | bytes 8192 | tf_op jit(solution)/shard_map/psum | solution.py:48
  288.7 252.1 %all-reduce.2.cloned.1.call-done = f32[64,2,8,128]{3,0,2,1:T(8,128)} async-done(((f32[64,2,8,128]{3,0,2,1:T(8,128)}), f32[64,2,8,128]{3,0,2,1:T(8,128)}) %all-reduce.2.cloned.1.call-update) | async-done | bytes 524304 | tf_op jit(solution)/shard_map/psum | solution.py:48
  540.8 1.2 divide_convert_fusion
  542.5 13.7 %psum.23 = bf16[64,256]{1,0:T(8,128)(2,1)S(1)} all-reduce(f32[64,256]{1,0:T(8,128)S(1)} %fusion.15), channel_id=1, replica_groups=mesh['seq'=32,'rep'=4,'tensor'=4] {'tensor'}, use_global_device_ids=true, to_apply=%region_9.10 | all-reduce | flops 16384 | bytes 98304 | tf_op jit(solution)/shard_map/psum | solution.py:51
  556.2 10.6 %all-gather = bf16[256,256]{1,0:T(8,128)(2,1)S(1)} all-gather(bf16[64,256]{1,0:T(8,128)(2,1)S(1)} %psum.23), channel_id=2, replica_groups=mesh['seq'=32,'rep'=4,'tensor'=4] {'rep'}, dimensions={0}, use_global_device_ids=true | all-gather | bytes 163840 | tf_op jit(solution)/shard_map/all_gather | solution.py:53
  566.9 1.3 select_bitcast_fusion.1
  (20 shorter events, 0.7 us)
Async XLA Ops:
  6.5 3.4 copy-start
  6.5 3.4 copy-start.3
  6.5 46.7 %all-gather.4.cloned.1.call-start = ((), (), s32[]{:S(2)}) async-start(), calls=%async_computation.1 | async-start | bytes 2621440 | tf_op jit(solution)/shard_map/all_gather | solution.py:25
  7.3 86.7 %all-gather.6.cloned.1.call-start = ((), (), s32[]{:S(2)}) async-start(), calls=%async_computation.2 | async-start | bytes 1310720 | tf_op jit(solution)/shard_map/all_gather | solution.py:15
  57.1 4.5 copy-start.4
  57.1 39.1 %all-to-all-start = ((bf16[384,4,2,256]{3,0,2,1:T(8,128)(2,1)}), bf16[384,4,2,256]{3,0,2,1:T(8,128)(2,1)}, u32[]{:S(2)}, u32[]{:S(2)}) async-start(bf16[384,4,2,256]{3,0,2,1:T(8,128)(2,1)} %bitcast.56), calls=%async_computation | async-start | bytes 3145728 | tf_op jit(solution)/shard_map/all_to_all | solution.py:33
  61.5 479.2 %all-reduce.2.cloned.1.call-start = ((), (), s32[]{:S(2)}) async-start(), calls=%async_computation.3 | async-start | bytes 1048576 | tf_op jit(solution)/shard_map/psum | solution.py:48
  97.7 3.7 copy-start.1
  193.0 349.2 %copy-start.2 = (bf16[2048,256]{1,0:T(8,128)(2,1)S(1)}, bf16[2048,256]{1,0:T(8,128)(2,1)}, u32[]{:S(2)}) copy-start(bf16[2048,256]{1,0:T(8,128)(2,1)} %param.12) | copy-start | bytes 3145732
Sparse Core Ops, SparseCore 0:
  9.5 43.7 all-gather.3
  55.4 38.5 all-gather.5
  191.9 348.8 all-reduce.1
where the time goes:
time: 579 us; the launch traced here: 575 us
  waiting for transfers between devices  327 us (56%)
  blocking collectives  201 us (35%)
  matrix products  13.7 us (2%)
  between operations  13.3 us (2%)
  other arithmetic  10.8 us (2%)
    psum x1, waiting for transfers between devices, shards(): summed, total = lax.psum((summed, total), 'seq')  252 us
    psum x1, blocking collectives, shards(): summed, total = lax.psum((summed, total), 'seq')  91.6 us
    pmax x1, blocking collectives, shards(): top = lax.pmax(jnp.max(scores, axis=-1), 'seq')  85.5 us
    all_gather x1, waiting for transfers between devices, shards(): complete_up_weight = lax.all_gather(w_up, 'tensor', axis=0, tiled=True)  42.3 us
    all_gather x1, waiting for transfers between devices, shards(): piece = lax.all_gather(queries, 'rep', axis=0, tiled=True)  31.2 us
    psum x1, blocking collectives, shards(): mixed = lax.psum(partial_output, 'tensor').astype(jnp.bfloat16)[None]  13.7 us
  transfers between devices with their start and end apart: 4, of which 3 were waited for; matrix products, arithmetic and copies ran while one was open for 3% of the time, Pallas kernels for 0%

commit v1 on v0

v1 whole, which is shorter than its diff:
```python
import functools
import math

import jax
import jax.numpy as jnp
from jax import lax
from jax.experimental import pallas as pl
from jax.experimental.pallas import tpu as pltpu
from jax.sharding import PartitionSpec as P

MESH = pl.DeviceIdType.MESH
F32 = jnp.float32
BF16 = jnp.bfloat16

TOK = 384
CH = 96
NCH = TOK // CH
HEADS = 16
NEW = 64
HD = 128
LAT = 512
COLS = 8 * NEW
C2 = math.log2(math.e) / math.sqrt(HD)


def dev(zhi, y, core, zlo, x):
    return (zhi * 8 + y * 2 + core, zlo, x)


def three(row):
    hi = row.astype(BF16).astype(F32)
    mid = (row - hi).astype(BF16).astype(F32)
    low = row - hi - mid
    zero = jnp.zeros((13, row.shape[1]), F32)
    return jnp.concatenate([hi, mid, low, zero], axis=0).astype(BF16)


def merge(parts):
    top = functools.reduce(jnp.maximum, [t for _, t in parts])
    scale = [jnp.exp2(t - top) for _, t in parts]
    total = functools.reduce(jnp.add, scale)
    inv = 1.0 / total
    value = functools.reduce(jnp.add, [v * (s * inv) for (v, _), s in zip(parts, scale)])
    return value, top + jnp.log2(total)


def unpack(ref, rows):
    value = ref[:rows].astype(F32)
    tail = ref[rows:].astype(F32)
    return value, tail[0:1] + tail[1:2] + tail[2:3]


def kernel(
    kv_hbm, q_hbm, wc_hbm, gain_ref, wup_hbm, wout_hbm, order_ref, out_ref,
    kv, kvf, wc, wup, wout, lat, qbuf, qf, qt, m_ref, l_ref, o_ref,
    send1, recv1, send2, recv2, zbuf, ycbuf, xbuf, zstage,
    kv_sem, w_sem, lat_ss, lat_rs, q_ss, q_rs, s1, r1, s2, r2, s3, r3, s4, r4, s5, r5,
):
    seq = lax.axis_index("seq")
    zlo = lax.axis_index("rep")
    x = lax.axis_index("tensor")
    zhi = seq // 8
    yc = seq % 8
    y = yc // 2
    core = yc % 2
    z = zhi * 4 + zlo

    def at_x(step):
        return (seq, zlo, (x + step) % 4)

    def at_z(step):
        there = (z + step) % 16
        return ((there // 4) * 8 + yc, there % 4, x)

    def at_yc(step):
        return (zhi * 8 + (yc + step) % 8, zlo, x)

    barrier = pltpu.get_barrier_semaphore()
    peers = [at_x(k) for k in range(1, 4)] + [at_z(k) for k in range(1, 16)] + [at_yc(k) for k in range(1, 8)]
    for peer in peers:
        pl.semaphore_signal(barrier, inc=1, device_id=peer, device_id_type=MESH)

    kv_in = [pltpu.make_async_copy(kv_hbm.at[pl.ds(c * CH, CH)], kv.at[c], kv_sem.at[c]) for c in range(NCH)]
    wc_in = pltpu.make_async_copy(wc_hbm, wc, w_sem.at[0])
    wup_in = pltpu.make_async_copy(wup_hbm, wup, w_sem.at[1])
    wout_in = pltpu.make_async_copy(wout_hbm, wout, w_sem.at[2])
    q_in = pltpu.make_async_copy(q_hbm, qbuf.at[0], w_sem.at[3])
    kv_in[0].start()
    wc_in.start()
    for c in range(1, NCH):
        kv_in[c].start()
    wup_in.start()
    q_in.start()
    wout_in.start()

    pl.semaphore_wait(barrier, len(peers))

    q_copies = []
    for n, (step, slot) in enumerate(((1, 3), (-1, 1))):
        q_copies.append(pltpu.make_async_remote_copy(
            src_ref=q_hbm, dst_ref=qbuf.at[slot], send_sem=q_ss.at[n], recv_sem=q_rs.at[n],
            device_id=at_z(step), device_id_type=MESH))
    for copy in q_copies:
        copy.start()

    def own_copy(c, way):
        return pltpu.make_async_remote_copy(
            src_ref=lat.at[c // 2, c % 2],
            dst_ref=lat.at[2 + way + 2 * (c // 2), c % 2],
            send_sem=lat_ss.at[4 * way + c],
            recv_sem=lat_rs.at[4 * way + c],
            device_id=at_x(1 if way == 0 else -1),
            device_id_type=MESH,
        )

    def pass_on(c):
        way = 0 if c < 2 else 1
        return pltpu.make_async_remote_copy(
            src_ref=lat.at[2 + way + 2 * (c // 2), c % 2],
            dst_ref=lat.at[6 + c // 2, c % 2],
            send_sem=lat_ss.at[8 + c],
            recv_sem=lat_rs.at[8 + c],
            device_id=at_x(1 if way == 0 else -1),
            device_id_type=MESH,
        )

    wc_in.wait()

    def compress(c, carry):
        pltpu.make_async_copy(kv_hbm.at[pl.ds(c * CH, CH)], kv.at[c], kv_sem.at[c]).wait()
        wide = kv[c].astype(F32).reshape(CH * 8, 2 * HD)
        for part in range(2):
            kvf[part] = wide[:, part * HD:(part + 1) * HD]
        rows = jnp.concatenate(
            [kvf[part, pl.ds(g, CH, stride=8), :].astype(BF16) for g in range(8) for part in range(2)], axis=1)
        projected = jnp.dot(rows, wc[...], preferred_element_type=F32)
        scale = lax.rsqrt(jnp.mean(projected * projected, axis=-1, keepdims=True) + 1e-06)
        lat[c // 2, c % 2] = (projected * scale * gain_ref[...].astype(F32)).astype(BF16)
        own_copy(c, 0).start()
        own_copy(c, 1).start()
        return carry

    lax.fori_loop(0, NCH, compress, 0)

    for c in (0, 1):
        own_copy(c, 0).wait_recv()
        pass_on(c).start()

    q_pass = []
    for n, (slot, step) in enumerate(((3, 1), (1, -1))):
        q_copies[n].wait_recv()
        half = pl.ds(n * (NEW // 2), NEW // 2)
        copy = pltpu.make_async_remote_copy(
            src_ref=qbuf.at[slot, half], dst_ref=qbuf.at[2, half],
            send_sem=q_ss.at[2 + n], recv_sem=q_rs.at[2 + n],
            device_id=at_z(step), device_id_type=MESH)
        copy.start()
        q_pass.append(copy)

    for c in (2, 3):
        own_copy(c, 1).wait_recv()
        pass_on(c).start()

    q_in.wait()
    for copy in q_pass:
        copy.wait_recv()

    source = jnp.int32(0)
    for r in range(4):
        source = source + jnp.where(order_ref[r] == zlo, r, 0)
    pick = (source - zlo + 4) % 4
    qf[...] = qbuf[pick].astype(F32).reshape(NEW * HEADS, HD)
    for pair in range(HEADS // 2):
        two = jnp.concatenate(
            [qf[pl.ds(2 * pair + h, NEW, stride=HEADS), :] for h in range(2)], axis=0)
        qt[pair // 4, :, (pair % 4) * 128:(pair % 4 + 1) * 128] = two.T.astype(BF16)

    wup_in.wait()
    m_ref[...] = jnp.full(m_ref.shape, -1e30, F32)
    l_ref[...] = jnp.zeros(l_ref.shape, F32)
    o_ref[...] = jnp.zeros(o_ref.shape, F32)

    def attend(i, carry):
        @pl.when(i == 3)
        def _():
            own_copy(0, 1).wait_recv()
            own_copy(1, 1).wait_recv()

        @pl.when(i == 4)
        def _():
            own_copy(2, 0).wait_recv()
            own_copy(3, 0).wait_recv()

        @pl.when(i == 6)
        def _():
            pass_on(0).wait_recv()
            pass_on(1).wait_recv()

        @pl.when(i == 7)
        def _():
            pass_on(2).wait_recv()
            pass_on(3).wait_recv()

        state = lat[i].reshape(2 * CH, LAT)
        for g in range(2):
            lifted = jnp.dot(state, wup[g], preferred_element_type=F32).astype(BF16)
            keys = lifted[:, :HD]
            values = lifted[:, HD:]
            scores = jnp.dot(keys, qt[g], preferred_element_type=F32)
            old = m_ref[g]
            top = jnp.maximum(old, jnp.max(scores, axis=0, keepdims=True))
            expo = jnp.exp2((scores - top) * C2)
            fade = jnp.exp2((old - top) * C2)
            l_ref[g] = l_ref[g] * fade + jnp.sum(expo, axis=0, keepdims=True)
            m_ref[g] = top
            o_ref[g] = o_ref[g] * fade + lax.dot_general(
                values, expo.astype(BF16), (((0,), (0,)), ((), ())), preferred_element_type=F32)
        return carry

    lax.fori_loop(0, 8, attend, 0)

    for g in range(2):
        total = l_ref[g]
        value = o_ref[g] * (1.0 / total)
        tail = three(m_ref[g] * C2 + jnp.log2(total))
        for k in range(4):
            cols = slice(128 * k, 128 * (k + 1))
            send1[4 * g + k, :HD] = value[:, cols].astype(BF16)
            send1[4 * g + k, HD:] = tail[:, cols]

    def scatter1(k):
        return pltpu.make_async_remote_copy(
            src_ref=send1.at[(yc + k) % 8], dst_ref=recv1.at[k - 1],
            send_sem=s1.at[k - 1], recv_sem=r1.at[k - 1],
            device_id=at_yc(k), device_id_type=MESH)

    for k in range(1, 8):
        scatter1(k).start()
    parts = [unpack(send1.at[yc], HD)]
    for k in range(1, 8):
        scatter1(k).wait_recv()
        parts.append(unpack(recv1.at[k - 1], HD))
    value, level = merge(parts)

    tail = three(level)
    for k in range(4):
        send2[k, :32] = value[32 * k:32 * (k + 1)].astype(BF16)
        send2[k, 32:] = tail

    def scatter2(k):
        return pltpu.make_async_remote_copy(
            src_ref=send2.at[(zhi + k) % 4], dst_ref=recv2.at[k - 1],
            send_sem=s2.at[k - 1], recv_sem=r2.at[k - 1],
            device_id=at_z(4 * k), device_id_type=MESH)

    for k in range(1, 4):
        scatter2(k).start()
    parts = [unpack(send2.at[zhi], 32)]
    for k in range(1, 4):
        scatter2(k).wait_recv()
        parts.append(unpack(recv2.at[k - 1], 32))
    value, _ = merge(parts)

    zstage[...] = value.astype(BF16)
    zbuf[z] = value.astype(BF16)

    def spread_z(k):
        return pltpu.make_async_remote_copy(
            src_ref=zstage, dst_ref=zbuf.at[z],
            send_sem=s3.at[k - 1], recv_sem=r3.at[k - 1],
            device_id=at_z(k), device_id_type=MESH)

    for k in range(1, 16):
        spread_z(k).start()
    for k in range(1, 16):
        spread_z(k).wait_recv()

    wanted = order_ref[zlo]
    mine = jnp.concatenate([zbuf[4 * q + wanted] for q in range(4)], axis=0)
    ycbuf[yc] = mine

    def spread_yc(k):
        return pltpu.make_async_remote_copy(
            src_ref=ycbuf.at[yc], dst_ref=ycbuf.at[yc],
            send_sem=s4.at[k - 1], recv_sem=r4.at[k - 1],
            device_id=at_yc(k), device_id_type=MESH)

    for k in range(1, 8):
        spread_yc(k).start()
    for k in range(1, 8):
        spread_yc(k).wait_recv()

    wout_in.wait()
    rows = []
    for j in range(8):
        part = ycbuf[j].astype(F32).T.astype(BF16)
        rows += [part[:NEW], part[NEW:]]
    partial = jnp.dot(jnp.concatenate(rows, axis=1), wout[...], preferred_element_type=F32)

    xbuf[0] = partial.astype(BF16)

    def spread_x(k):
        return pltpu.make_async_remote_copy(
            src_ref=xbuf.at[0], dst_ref=xbuf.at[k],
            send_sem=s5.at[k - 1], recv_sem=r5.at[k - 1],
            device_id=at_x(k), device_id_type=MESH)

    for k in range(1, 4):
        spread_x(k).start()
    for k in range(1, 4):
        spread_x(k).wait_recv()
        partial = partial + xbuf[k].astype(F32)
    out_ref[0] = partial.astype(BF16)

    for c in range(NCH):
        own_copy(c, 0).wait_send()
        own_copy(c, 1).wait_send()
        pass_on(c).wait_send()
    for copy in q_copies + q_pass:
        copy.wait_send()
    for k in range(1, 8):
        scatter1(k).wait_send()
        spread_yc(k).wait_send()
    for k in range(1, 4):
        scatter2(k).wait_send()
        spread_x(k).wait_send()
    for k in range(1, 16):
        spread_z(k).wait_send()


def shards(key_value_rows, queries, w_comp, latent_gain, w_up, w_out, replica_order):
    dma = lambda n: pltpu.SemaphoreType.DMA((n,))
    anywhere = pl.BlockSpec(memory_space=pl.ANY)
    vmem = pl.BlockSpec(memory_space=pltpu.VMEM)
    smem = pl.BlockSpec(memory_space=pltpu.SMEM)
    return pl.pallas_call(
        kernel,
        out_shape=jax.ShapeDtypeStruct((1, NEW, 256), BF16),
        in_specs=[anywhere, anywhere, anywhere, vmem, anywhere, anywhere, smem],
        out_specs=vmem,
        scratch_shapes=[
            pltpu.VMEM((NCH, CH, 8, 2 * HD), BF16),
            pltpu.VMEM((2, CH * 8, HD), F32),
            pltpu.VMEM((2048, LAT), BF16),
            pltpu.VMEM((2, LAT, 2 * HD), BF16),
            pltpu.VMEM((2048, 256), BF16),
            pltpu.VMEM((8, 2, CH, LAT), BF16),
            pltpu.VMEM((4, NEW, HEADS, HD), BF16),
            pltpu.VMEM((NEW * HEADS, HD), F32),
            pltpu.VMEM((2, HD, COLS), BF16),
            pltpu.VMEM((2, 1, COLS), F32),
            pltpu.VMEM((2, 1, COLS), F32),
            pltpu.VMEM((2, HD, COLS), F32),
            pltpu.VMEM((8, HD + 16, 128), BF16),
            pltpu.VMEM((7, HD + 16, 128), BF16),
            pltpu.VMEM((4, 48, 128), BF16),
            pltpu.VMEM((3, 48, 128), BF16),
            pltpu.VMEM((16, 32, 128), BF16),
            pltpu.VMEM((8, HD, 128), BF16),
            pltpu.VMEM((4, NEW, 256), BF16),
            pltpu.VMEM((32, 128), BF16),
            dma(NCH), dma(4), dma(12), dma(12), dma(4), dma(4),
            dma(7), dma(7), dma(3), dma(3), dma(15), dma(15), dma(7), dma(7), dma(3), dma(3),
        ],
        compiler_params=pltpu.CompilerParams(
            collective_id=0, has_side_effects=True, vmem_limit_bytes=63 * 1024 * 1024),
        cost_estimate=pl.CostEstimate(flops=3_000_000_000, bytes_accessed=7_000_000, transcendentals=1_600_000),
    )(key_value_rows[0], queries[0], w_comp, latent_gain.reshape(1, LAT), w_up, w_out, replica_order)


def solution(mesh):
    placed = (
        P("rep", ("seq", "tensor"), None, None),
        P("rep", None, "tensor", None),
        P(),
        P(),
        P("tensor", None, None),
        P("tensor", "seq"),
        P(),
    )
    return jax.shard_map(
        shards, mesh=mesh, in_specs=placed, out_specs=P("rep", None, "seq"), check_vma=False
    )
```

time: 579 us -> 74.8 us (0.13)
  waiting for transfers between devices: 327 us -> 0 us
  blocking collectives: 201 us -> 0 us
  Pallas kernels: 0 us -> 72 us
  matrix products: 13.7 us -> 0 us
  between operations: 13.3 us -> 0.01 us
  other arithmetic: 10.8 us -> 0 us
    psum x1 -> x0, waiting for transfers between devices: 252 us -> none  [shards(): summed, total = lax.psum((summed, total), 'seq')]
    psum x2 -> x0, blocking collectives: 105 us -> none  [the longest x1 91.6 us: shards(): summed, total = lax.psum((summed, total), 'seq')]
    pmax x1 -> x0, blocking collectives: 85.5 us -> none  [shards(): top = lax.pmax(jnp.max(scores, axis=-1), 'seq')]
    all_gather x2 -> x0, waiting for transfers between devices: 73.4 us -> none  [the longest x1 42.3 us: shards(): complete_up_weight = lax.all_gather(w_up, 'tensor', axis=0, tiled=True)]
    pallas_call x0 -> x1, Pallas kernels: none -> 72 us  [shards(): pl.pallas_call(kernel, out_shape=jax.ShapeDtypeStruct((1, NEW, 256), BF16...]
    dot_general x5 -> x0, matrix products: 13.7 us -> none  [the longest x1 4.93 us: shards(): jnp.einsum('nght,tgd->nghd', weights, values, preferred_element_type=jnp....]
    all_gather x1 -> x0, blocking collectives: 10.6 us -> none  [shards(): piece = lax.all_gather(mixed, 'rep', axis=0, tiled=True)]
  transfers between devices with their start and end apart: 4 -> 0, of which waited for: 3 -> 0; matrix products, arithmetic and copies ran while one was open for 3% -> 0% of each run, Pallas kernels for 0% -> 0%
where the time goes in v1:
time: 74.8 us; the launch traced here: 74.6 us
  Pallas kernels  72 us (96%)
  local copies, waits for them, and re-layouts  2.63 us (4%)
    pallas_call x1, Pallas kernels, shards(): pl.pallas_call(kernel, out_shape=jax.ShapeDtypeStruct((1, NEW, 256), BF16...  72 us

profile of v1, /device:TPU:1, one launch (start us, length us, event | category | flops | bytes accessed | tf_op | source)
XLA Modules:
  0.0 74.6 jit_solution(933572204006000891)
XLA Ops:
  0.0 1.3 %reshape.3.gain_ref = bf16[1,512]{1,0:T(2,128)(2,1)} reshape(bf16[512]{0:T(512)(128)(2,1)} %param.10) | data formatting | bytes 2048 | tf_op jit(solution)/shard_map/reshape | solution.py:368
  1.3 72.0 %shard_map.73 = bf16[1,64,256]{2,1,0:T(8,128)(2,1)} custom-call(bf16[384,8,256]{2,1,0:T(8,128)(2,1)} %bitcast.2, bf16[64,16,128]{2,1,0:T(8,128)(2,1)} %bitcast.3, bf16[2048,512]{1,0:T(8,128)(2,1)} %wc_hbm.1, bf16[1,512]{1,0:T(2,128)(2,1)} %reshape.3.gain_ref, bf16[2,512,256]{2,1,0:T(8,128)(2,1)} %wup_hbm.1, bf16[2048,256]{1,0:T(8,128)(2,1)} %wout_hbm.1, ...), custom_call_target="tpu_custom_call" | custom-call | flops 3000000000 | bytes 7000000 | tf_op jit(solution)/shard_map/pallas_call | solution.py:336
  73.2 1.4 %copy.9 = bf16[1,64,256]{2,1,0:T(8,128)(2,1)} copy(bf16[1,64,256]{2,1,0:T(8,128)(2,1)} %shard_map.73) | data formatting | bytes 65536

commit v2 on v0

v2 whole, which is shorter than its diff:
```python
import functools
import math

import jax
import jax.numpy as jnp
from jax import lax
from jax.experimental import pallas as pl
from jax.experimental.pallas import tpu as pltpu
from jax.sharding import PartitionSpec as P

MESH = pl.DeviceIdType.MESH
F32 = jnp.float32
BF16 = jnp.bfloat16

TOK = 384
CH = 96
NCH = TOK // CH
NEW = 64
HD = 128
LAT = 512
COLS = 8 * NEW
C2 = math.log2(math.e) / math.sqrt(HD)


def three(row):
    hi = row.astype(BF16).astype(F32)
    mid = (row - hi).astype(BF16).astype(F32)
    low = row - hi - mid
    zero = jnp.zeros((13, row.shape[1]), F32)
    return jnp.concatenate([hi, mid, low, zero], axis=0).astype(BF16)


def merge(parts):
    top = functools.reduce(jnp.maximum, [t for _, t in parts])
    scale = [jnp.exp2(t - top) for _, t in parts]
    total = functools.reduce(jnp.add, scale)
    inv = 1.0 / total
    value = functools.reduce(jnp.add, [v * (s * inv) for (v, _), s in zip(parts, scale)])
    return value, top + jnp.log2(total)


def unpack(ref, rows):
    value = ref[:rows].astype(F32)
    tail = ref[rows:].astype(F32)
    return value, tail[0:1] + tail[1:2] + tail[2:3]


def kernel(
    kv_hbm, q_hbm, wc_hbm, gain_ref, wup_hbm, wout_hbm, order_ref, out_ref,
    kv, kvf, wc, wup, wout, lat, qbuf, qf, qt, m_ref, l_ref, o_ref,
    send1, recv1, send2, recv2, heads, xbuf, zbuf,
    kv_sem, w_sem, lat_ss, lat_rs, sib_ss, sib_rs, q_ss, q_rs, s1, r1, s2, r2, s3, r3, s4, r4, s5, r5, far,
):
    seq = lax.axis_index("seq")
    zlo = lax.axis_index("rep")
    x = lax.axis_index("tensor")
    zhi = seq // 8
    y = seq % 8 // 2
    core = seq % 2
    z = zhi * 4 + zlo

    def at_x(step):
        return (seq, zlo, (x + step + 4) % 4)

    def at_y(step):
        return (zhi * 8 + (y + step) % 4 * 2 + core, zlo, x)

    def at_z(step):
        there = (z + step + 16) % 16
        return (there // 4 * 8 + y * 2 + core, there % 4, x)

    def at_zlo(step):
        return (seq, (zlo + step) % 4, x)

    sibling = (zhi * 8 + y * 2 + 1 - core, zlo, x)

    def copy_to(device, src, dst, send_sem, recv_sem):
        return pltpu.make_async_remote_copy(
            src_ref=src, dst_ref=dst, send_sem=send_sem, recv_sem=recv_sem,
            device_id=device, device_id_type=MESH)

    barrier = pltpu.get_barrier_semaphore()
    near = [sibling] + [at_x(k) for k in (1, 2, 3)] + [at_y(k) for k in (1, 2, 3)]
    near += [at_zlo(k) for k in (1, 2, 3)] + [at_z(k) for k in (1, -1)]
    for peer in near:
        pl.semaphore_signal(barrier, inc=1, device_id=peer, device_id_type=MESH)

    kv_in = [pltpu.make_async_copy(kv_hbm.at[pl.ds(c * CH, CH)], kv.at[c], kv_sem.at[c]) for c in range(NCH)]
    wc_in = pltpu.make_async_copy(wc_hbm, wc, w_sem.at[0])
    wup_in = pltpu.make_async_copy(wup_hbm.at[core], wup, w_sem.at[1])
    wout_in = pltpu.make_async_copy(wout_hbm, wout, w_sem.at[2])
    q_here = q_hbm.at[:, pl.ds(core * 8, 8)]
    q_in = pltpu.make_async_copy(q_here, qbuf.at[0], w_sem.at[3])
    kv_in[0].start()
    wc_in.start()
    for c in range(1, NCH):
        kv_in[c].start()
    q_in.start()
    wup_in.start()
    wout_in.start()

    pl.semaphore_wait(barrier, len(near))

    def tell(n, step):
        for way in (1, -1):
            pl.semaphore_signal(far.at[n], inc=1, device_id=at_z(way * step), device_id_type=MESH)

    tell(0, 1)

    def half(n):
        return pl.ds(n * (NEW // 2), NEW // 2)

    def q_send(way, n):
        slot = (3, 1)[way]
        return copy_to(
            at_z((1, -1)[way]), q_hbm.at[half(n), pl.ds(core * 8, 8)], qbuf.at[slot, half(n)],
            q_ss.at[2 * way + n], q_rs.at[2 * way + n])

    def q_pass(way):
        return copy_to(
            at_z((1, -1)[way]), qbuf.at[(3, 1)[way], half(way)], qbuf.at[2, half(way)],
            q_ss.at[4 + way], q_rs.at[4 + way])

    for n in range(2):
        q_send(0, n).start()
        q_send(1, 1 - n).start()
    sent = [q_send(way, n) for way in range(2) for n in range(2)]

    def first(c):
        return copy_to(
            at_x(1 - 2 * (c % 2)), lat.at[c, core], lat.at[4 + c, core], lat_ss.at[c], lat_rs.at[4 + c])

    def second(c):
        there = 9 + c - 2 * (c % 2)
        return copy_to(
            at_x(2 * (c % 2) - 1), lat.at[c, core], lat.at[there, core], lat_ss.at[4 + c], lat_rs.at[there])

    def pass_on(s):
        return copy_to(
            at_x(1 - 2 * (s % 2)), lat.at[s, core], lat.at[s + 8, core], lat_ss.at[4 + s], lat_rs.at[s + 8])

    def share(s):
        return copy_to(sibling, lat.at[s, core], lat.at[s, core], sib_ss.at[s], sib_rs.at[s])

    def arrive(s):
        copy_to(sibling, lat.at[s, core], lat.at[s, core], sib_ss.at[s], lat_rs.at[s]).wait_recv()

    wc_in.wait()

    def compress(c, carry):
        pltpu.make_async_copy(kv_hbm.at[pl.ds(c * CH, CH)], kv.at[c], kv_sem.at[c]).wait()
        wide = kv[c].astype(F32).reshape(CH * 8, 2 * HD)
        for part in range(2):
            kvf[part] = wide[:, part * HD:(part + 1) * HD]
        rows = jnp.concatenate(
            [kvf[part, pl.ds(g, CH, stride=8), :].astype(BF16) for g in range(8) for part in range(2)], axis=1)
        projected = jnp.dot(rows, wc[...], preferred_element_type=F32)
        scale = lax.rsqrt(jnp.mean(projected * projected, axis=-1, keepdims=True) + 1e-06)
        gain = gain_ref[...].astype(F32).reshape(1, LAT)
        lat[c, core] = (projected * scale * gain).astype(BF16)
        first(c).start()
        share(c).start()
        return carry

    lax.fori_loop(0, NCH, compress, 0)
    for c in (1, 0, 3, 2):
        second(c).start()
    sent += [first(c) for c in range(4)] + [second(c) for c in range(4)]

    pl.semaphore_wait(far.at[0], 2)
    tell(1, 2)
    for way in range(2):
        q_send(way, way).wait_recv()
        q_pass(way).start()
    sent += [q_pass(way) for way in range(2)]

    def relay(s, carry):
        arrive(s)
        pass_on(s).start()
        share(s).start()
        return carry

    lax.fori_loop(4, 8, relay, 0)
    sent += [pass_on(s) for s in range(4, 8)] + [share(s) for s in range(16)]

    pl.semaphore_wait(far.at[1], 2)
    tell(2, 4)
    q_in.wait()
    for way in range(2):
        q_send(way, 1 - way).wait_recv()
    for way in range(2):
        q_pass(way).wait_recv()

    source = jnp.int32(0)
    for r in range(4):
        source = source + jnp.where(order_ref[r] == zlo, r, 0)
    pick = (source - zlo + 4) % 4
    qf[...] = qbuf[pick].astype(F32).reshape(NEW * 8, HD)
    for pair in range(4):
        two = jnp.concatenate([qf[pl.ds(2 * pair + h, NEW, stride=8), :] for h in range(2)], axis=0)
        qt[:, pair * 128:(pair + 1) * 128] = two.T.astype(BF16)

    wup_in.wait()
    m_ref[...] = jnp.full(m_ref.shape, -1e30, F32)
    l_ref[...] = jnp.zeros(l_ref.shape, F32)
    o_ref[...] = jnp.zeros(o_ref.shape, F32)

    def attend(s, carry):
        for now, coming in ((4, 8), (5, 9), (6, 10), (7, 11), (10, 12), (11, 13), (13, 14), (14, 15)):
            @pl.when(s == now)
            def _():
                arrive(coming)
                share(coming).start()

        share(s).wait_recv()
        lifted = jnp.dot(
            lat[s].reshape(2 * CH, LAT), wup[...], preferred_element_type=F32).astype(BF16)
        keys = lifted[:, :HD]
        values = lifted[:, HD:]
        scores = jnp.dot(keys, qt[...], preferred_element_type=F32)
        old = m_ref[...]
        top = jnp.maximum(old, jnp.max(scores, axis=0, keepdims=True))
        expo = jnp.exp2((scores - top) * C2)
        fade = jnp.exp2((old - top) * C2)
        l_ref[...] = l_ref[...] * fade + jnp.sum(expo, axis=0, keepdims=True)
        m_ref[...] = top
        o_ref[...] = o_ref[...] * fade + lax.dot_general(
            values, expo.astype(BF16), (((0,), (0,)), ((), ())), preferred_element_type=F32)
        return carry

    lax.fori_loop(0, 16, attend, 0)

    total = l_ref[...]
    value = o_ref[...] * (1.0 / total)
    tail = three(m_ref[...] * C2 + jnp.log2(total))
    for k in range(4):
        cols = slice(128 * k, 128 * (k + 1))
        send1[k, :HD] = value[:, cols].astype(BF16)
        send1[k, HD:] = tail[:, cols]

    def scatter(k):
        return copy_to(at_y(k), send1.at[(y + k) % 4], recv1.at[k - 1], s1.at[k - 1], r1.at[k - 1])

    for k in (2, 1, 3):
        scatter(k).start()
    sent += [scatter(k) for k in (1, 2, 3)]
    parts = [unpack(send1.at[y], HD)]
    for k in (1, 3, 2):
        scatter(k).wait_recv()
        parts.append(unpack(recv1.at[k - 1], HD))
    value, level = merge(parts)

    send2[:HD] = value.astype(BF16)
    send2[HD:] = three(level)
    pl.semaphore_wait(far.at[2], 2)

    def across(k):
        return copy_to(at_z(4 * k), send2, recv2.at[k - 1], s2.at[k - 1], r2.at[k - 1])

    for k in (2, 1, 3):
        across(k).start()
    sent += [across(k) for k in (1, 2, 3)]
    parts = [unpack(send2, HD)]
    for k in (1, 3, 2):
        across(k).wait_recv()
        parts.append(unpack(recv2.at[k - 1], HD))
    value, _ = merge(parts)

    heads[core, y] = value.T.astype(BF16)

    def spread(k):
        return copy_to(at_y(k), heads.at[core, y], heads.at[core, y], s3.at[k], r3.at[k])

    def pair(k):
        there = heads.at[core, (y - k + 4) % 4]
        return copy_to(sibling, there, there, s3.at[4 + k], r3.at[4 + k])

    for k in (2, 1, 3):
        spread(k).start()
    pair(0).start()
    for k in (1, 3, 2):
        spread(k).wait_recv()
        pair(k).start()
    for k in range(4):
        pair(k).wait_recv()
    sent += [spread(k) for k in (1, 2, 3)] + [pair(k) for k in range(4)]

    wout_in.wait()
    rows = [heads[g, k, h * NEW:(h + 1) * NEW] for g in range(2) for k in range(4) for h in range(2)]
    partial = jnp.dot(jnp.concatenate(rows, axis=1), wout[...], preferred_element_type=F32)

    xbuf[0] = partial.astype(BF16)

    def add_x(k):
        return copy_to(at_x(k), xbuf.at[0], xbuf.at[k], s4.at[k - 1], r4.at[k - 1])

    for k in (2, 1, 3):
        add_x(k).start()
    sent += [add_x(k) for k in (1, 2, 3)]
    for k in (1, 3, 2):
        add_x(k).wait_recv()
        partial = partial + xbuf[k].astype(F32)

    zbuf[0] = partial.astype(BF16)

    def reply(k):
        return copy_to(at_zlo(k), zbuf.at[0], zbuf.at[k], s5.at[k - 1], r5.at[k - 1])

    for k in (2, 1, 3):
        reply(k).start()
    sent += [reply(k) for k in (1, 2, 3)]
    for k in (1, 3, 2):
        reply(k).wait_recv()
    out_ref[0] = zbuf[(zlo - order_ref[zlo] + 4) % 4]

    for copy in sent:
        copy.wait_send()


def shards(key_value_rows, queries, w_comp, latent_gain, w_up, w_out, replica_order):
    dma = lambda n: pltpu.SemaphoreType.DMA((n,))
    anywhere = pl.BlockSpec(memory_space=pl.ANY)
    vmem = pl.BlockSpec(memory_space=pltpu.VMEM)
    smem = pl.BlockSpec(memory_space=pltpu.SMEM)
    return pl.pallas_call(
        kernel,
        out_shape=jax.ShapeDtypeStruct((1, NEW, 256), BF16),
        in_specs=[anywhere, anywhere, anywhere, vmem, anywhere, anywhere, smem],
        out_specs=vmem,
        scratch_shapes=[
            pltpu.VMEM((NCH, CH, 8, 2 * HD), BF16),
            pltpu.VMEM((2, CH * 8, HD), F32),
            pltpu.VMEM((2048, LAT), BF16),
            pltpu.VMEM((LAT, 2 * HD), BF16),
            pltpu.VMEM((2048, 256), BF16),
            pltpu.VMEM((16, 2, CH, LAT), BF16),
            pltpu.VMEM((4, NEW, 8, HD), BF16),
            pltpu.VMEM((NEW * 8, HD), F32),
            pltpu.VMEM((HD, COLS), BF16),
            pltpu.VMEM((1, COLS), F32),
            pltpu.VMEM((1, COLS), F32),
            pltpu.VMEM((HD, COLS), F32),
            pltpu.VMEM((4, HD + 16, 128), BF16),
            pltpu.VMEM((3, HD + 16, 128), BF16),
            pltpu.VMEM((HD + 16, 128), BF16),
            pltpu.VMEM((3, HD + 16, 128), BF16),
            pltpu.VMEM((2, 4, 2 * NEW, HD), BF16),
            pltpu.VMEM((4, NEW, 256), BF16),
            pltpu.VMEM((4, NEW, 256), BF16),
            dma(NCH), dma(4), dma(12), dma(16), dma(16), dma(16), dma(6), dma(6),
            dma(3), dma(3), dma(3), dma(3), dma(8), dma(8), dma(3), dma(3), dma(3), dma(3),
            pltpu.SemaphoreType.REGULAR((3,)),
        ],
        compiler_params=pltpu.CompilerParams(
            collective_id=0, has_side_effects=True, vmem_limit_bytes=63 * 1024 * 1024),
        cost_estimate=pl.CostEstimate(flops=3_000_000_000, bytes_accessed=7_000_000, transcendentals=1_600_000),
    )(key_value_rows[0], queries[0], w_comp, latent_gain, w_up, w_out, replica_order)


def solution(mesh):
    placed = (
        P("rep", ("seq", "tensor"), None, None),
        P("rep", None, "tensor", None),
        P(),
        P(),
        P("tensor", None, None),
        P("tensor", "seq"),
        P(),
    )
    return jax.shard_map(
        shards, mesh=mesh, in_specs=placed, out_specs=P("rep", None, "seq"), check_vma=False
    )
```

time: 579 us -> 67 us (0.12)
  waiting for transfers between devices: 327 us -> 0 us
  blocking collectives: 201 us -> 0 us
  Pallas kernels: 0 us -> 65.4 us
  matrix products: 13.7 us -> 0 us
  between operations: 13.3 us -> 0.01 us
  other arithmetic: 10.8 us -> 0 us
    psum x1 -> x0, waiting for transfers between devices: 252 us -> none  [shards(): summed, total = lax.psum((summed, total), 'seq')]
    psum x2 -> x0, blocking collectives: 105 us -> none  [the longest x1 91.6 us: shards(): summed, total = lax.psum((summed, total), 'seq')]
    pmax x1 -> x0, blocking collectives: 85.5 us -> none  [shards(): top = lax.pmax(jnp.max(scores, axis=-1), 'seq')]
    all_gather x2 -> x0, waiting for transfers between devices: 73.4 us -> none  [the longest x1 42.3 us: shards(): complete_up_weight = lax.all_gather(w_up, 'tensor', axis=0, tiled=True)]
    pallas_call x0 -> x1, Pallas kernels: none -> 65.4 us  [shards(): pl.pallas_call(kernel, out_shape=jax.ShapeDtypeStruct((1, NEW, 256), BF16...]
    dot_general x5 -> x0, matrix products: 13.7 us -> none  [the longest x1 4.93 us: shards(): jnp.einsum('nght,tgd->nghd', weights, values, preferred_element_type=jnp....]
    all_gather x1 -> x0, blocking collectives: 10.6 us -> none  [shards(): piece = lax.all_gather(mixed, 'rep', axis=0, tiled=True)]
  transfers between devices with their start and end apart: 4 -> 0, of which waited for: 3 -> 0; matrix products, arithmetic and copies ran while one was open for 3% -> 0% of each run, Pallas kernels for 0% -> 0%
where the time goes in v2:
time: 67 us; the launch traced here: 66.8 us
  Pallas kernels  65.4 us (98%)
  local copies, waits for them, and re-layouts  1.38 us (2%)
    pallas_call x1, Pallas kernels, shards(): pl.pallas_call(kernel, out_shape=jax.ShapeDtypeStruct((1, NEW, 256), BF16...  65.4 us
    unnamed x1, local copies, waits for them, and re-layouts  1.38 us

profile of v2, /device:TPU:1, one launch (start us, length us, event | category | flops | bytes accessed | tf_op | source)
XLA Modules:
  0.0 66.8 jit_solution(1928448435243229182)
XLA Ops:
  0.0 65.4 %shard_map.73 = bf16[1,64,256]{2,1,0:T(8,128)(2,1)} custom-call(bf16[384,8,256]{2,1,0:T(8,128)(2,1)} %bitcast.2, bf16[64,16,128]{2,1,0:T(8,128)(2,1)} %bitcast.3, bf16[2048,512]{1,0:T(8,128)(2,1)} %wc_hbm.1, bf16[512]{0:T(512)(128)(2,1)} %gain_ref.1, bf16[2,512,256]{2,1,0:T(8,128)(2,1)} %wup_hbm.1, bf16[2048,256]{1,0:T(8,128)(2,1)} %wout_hbm.1, s32[4]{0:T(128)} %order_ref.1), custom_call_target="tpu_custom_call" | custom-call | flops 3000000000 | bytes 7000000 | tf_op jit(solution)/shard_map/pallas_call | solution.py:325
  65.4 1.4 %copy.9 = bf16[1,64,256]{2,1,0:T(8,128)(2,1)} copy(bf16[1,64,256]{2,1,0:T(8,128)(2,1)} %shard_map.73) | data formatting | bytes 65536
